TPU v7x, 32 devices: a whole 2x2x4 slice. The times are simulated.
32 devices in a mesh: ctx: 8 (over y, x, core), exp: 4 (over z).
Axes of the slice: x: 2, y: 2, z: 4, core: 2. Of those that a mesh axis runs over, the one named last changes fastest.
Arguments:
- hidden: bfloat16 [4096, 2048], P(('ctx', 'exp')), may hold values from -6 to 6
- queries: bfloat16 [4096, 2048], P(('ctx', 'exp')), may hold values from -16 to 16
- keys: bfloat16 [4096, 256], P(('ctx', 'exp')), may hold values from -4 to 4
- values: bfloat16 [4096, 256], P(('ctx', 'exp')), may hold values from -6 to 6
- w_out: bfloat16 [2048, 2048], replicated, may hold values from -0.125 to 0.125
- norm_gain: float32 [2048], replicated, may hold values from 0.5 to 1.5
- w_router: bfloat16 [2048, 128], replicated, may hold values from -0.125 to 0.125
- expert_ids: int32 [4096, 8], P(('ctx', 'exp')), may hold values from 0 to 127, all different within a row; in each aligned block of 128 rows (0 to 127, 128 to 255, ...) at most 9 rows name the same one
- w_gate: bfloat16 [128, 2048, 768], P(('ctx', 'exp')), may hold values from -0.125 to 0.125
- w_up: bfloat16 [128, 2048, 768], P(('ctx', 'exp')), may hold values from -0.125 to 0.125
- w_down: bfloat16 [128, 768, 2048], P(('ctx', 'exp')), may hold values from -0.21875 to 0.21875
Outputs:
- mixed: bfloat16 [4096, 2048], P(('ctx', 'exp'))
Inputs may be any that keep to these rules, and one draw needn't show every extreme that they name: `expert_ids`: within the 128 tokens of one device, no expert is named by more than 9 of their routes, a bound that some block reaches of them; a token's experts are distinct.
All inputs are finite; a program needn't handle non-finite values.
Results may differ from a plain program's by a relative error of at most 0.01.
Values may be sent and summed in bfloat16 or wider, within the bound.
A program may use at most 192 MiB of HBM per device.

v0:
```python
import math

import jax
import jax.numpy as jnp
from jax import lax
from jax.sharding import PartitionSpec as P

DH = 128
TOP = 8
CAP = 9


rope_base = 1000000.0
yarn_factor = 4.0
orig_len = 32768.0
beta_fast = 32.0
beta_slow = 1.0
mscale_yarn = 0.1 * math.log(4.0) + 1.0


def yarn_tables(positions, head_size):
    half_size = head_size // 2
    index_f = jnp.arange(half_size, dtype=jnp.float32)
    pos_freq = rope_base ** (2.0 * index_f / head_size)
    inv_extra = 1.0 / pos_freq
    inv_inter = 1.0 / (yarn_factor * pos_freq)
    low_dim = max(
        math.floor(
            head_size
            * math.log(orig_len / (beta_fast * 2.0 * math.pi))
            / (2.0 * math.log(rope_base))
        ),
        0,
    )
    high_dim = min(
        math.ceil(
            head_size
            * math.log(orig_len / (beta_slow * 2.0 * math.pi))
            / (2.0 * math.log(rope_base))
        ),
        head_size - 1,
    )
    ramp_part = jnp.clip((index_f - low_dim) / max(high_dim - low_dim, 0.001), 0.0, 1.0)
    extra_part = 1.0 - ramp_part
    inverse = inv_inter * (1.0 - extra_part) + inv_extra * extra_part
    angles = positions.astype(jnp.float32)[:, None] * inverse[None, :]
    angles = jnp.concatenate([angles, angles], axis=-1)
    return (jnp.cos(angles) * mscale_yarn, jnp.sin(angles) * mscale_yarn)


def rotate(vectors, cos_table, sin_table):
    values_f = vectors.astype(jnp.float32)
    half_size = values_f.shape[-1] // 2
    turned = jnp.concatenate([-values_f[..., half_size:], values_f[..., :half_size]], axis=-1)
    return (values_f * cos_table[:, None, :] + turned * sin_table[:, None, :]).astype(jnp.bfloat16)


def local(
    hidden, queries, keys, values, w_out, norm_gain, w_router, expert_ids, w_gate, w_up, w_down
):
    tok_rows = hidden.shape[0]
    kv_heads = keys.shape[1] // DH
    q_heads = queries.shape[1] // DH
    group = q_heads // kv_heads
    experts_all = w_router.shape[1]
    width = hidden.shape[1]
    device = lax.axis_index(("ctx", "exp"))
    first_row = device * tok_rows
    positions = first_row + jnp.arange(tok_rows, dtype=jnp.int32)
    cos_table, sin_table = yarn_tables(positions, DH)
    q_four = rotate(queries.reshape(tok_rows, q_heads, DH), cos_table, sin_table).reshape(
        tok_rows, kv_heads, group, DH
    )
    k_flat = rotate(keys.reshape(tok_rows, kv_heads, DH), cos_table, sin_table).reshape(
        tok_rows, kv_heads * DH
    )
    q_rows = first_row + jnp.arange(tok_rows, dtype=jnp.int32)
    scale = 1.0 / math.sqrt(DH)

    def update(carry, operands):
        run_max, run_sum, run_acc = carry
        key_block, value_block, block_start = operands
        block_len = key_block.shape[0]
        scores = (
            jnp.einsum("thgd,phd->thgp", q_four, key_block, preferred_element_type=jnp.float32)
            * scale
        )
        key_rows = block_start + jnp.arange(block_len, dtype=jnp.int32)
        allowed = (key_rows[None, :] <= q_rows[:, None])[:, None, None, :]
        scores = jnp.where(allowed, scores, -1e30)
        new_max = jnp.maximum(run_max, jnp.max(scores, axis=-1))
        weights = jnp.where(allowed, jnp.exp(scores - new_max[..., None]), 0.0)
        factor = jnp.exp(run_max - new_max)
        new_sum = run_sum * factor + jnp.sum(weights, axis=-1)
        added = jnp.einsum(
            "thgp,phd->thgd",
            weights.astype(jnp.bfloat16),
            value_block,
            preferred_element_type=jnp.float32,
        )
        return ((new_max, new_sum, run_acc * factor[..., None] + added), None)

    initial = (
        jnp.full((tok_rows, kv_heads, group), -1e30, jnp.float32),
        jnp.zeros((tok_rows, kv_heads, group), jnp.float32),
        jnp.zeros((tok_rows, kv_heads, group, DH), jnp.float32),
    )
    key_piece = lax.all_gather(k_flat, ("ctx", "exp"), axis=0, tiled=True)
    value_piece = lax.all_gather(values, ("ctx", "exp"), axis=0, tiled=True)
    piece_len = key_piece.shape[0]
    block_len = math.gcd(piece_len, 1024)
    count = piece_len // block_len
    key_blocks = key_piece.reshape(count, block_len, kv_heads, DH)
    value_blocks = value_piece.reshape(count, block_len, kv_heads, DH)
    offsets = jnp.arange(count, dtype=jnp.int32) * block_len
    result, unused = lax.scan(update, initial, (key_blocks, value_blocks, offsets))
    final_max, final_sum, final_acc = result
    attn = (final_acc / final_sum[..., None]).astype(jnp.bfloat16).reshape(tok_rows, q_heads * DH)
    h1 = (
        jnp.dot(attn, w_out, preferred_element_type=jnp.float32) + hidden.astype(jnp.float32)
    ).astype(jnp.bfloat16)
    h1_f = h1.astype(jnp.float32)
    normed = (
        h1_f / jnp.sqrt(jnp.mean(h1_f * h1_f, axis=-1, keepdims=True) + 1e-06) * norm_gain[None, :]
    )
    hn = normed.astype(jnp.bfloat16)
    logits = jnp.dot(hn, w_router, preferred_element_type=jnp.float32)
    onehot = expert_ids[:, :, None] == jnp.arange(experts_all, dtype=jnp.int32)[None, None, :]
    chosen = jnp.sum(jnp.where(onehot, logits[:, None, :], 0.0), axis=-1)
    raised = jnp.exp(chosen)
    route_w = (raised / jnp.sum(raised, axis=-1, keepdims=True)).astype(jnp.bfloat16)
    counts = jnp.cumsum(
        onehot.reshape(tok_rows * TOP, experts_all).astype(jnp.int32), axis=0
    ).reshape(tok_rows, TOP, experts_all)
    slot = jnp.sum(jnp.where(onehot, counts, 0), axis=-1) - 1
    target = expert_ids * CAP + slot
    slot_ids = jnp.arange(experts_all * CAP, dtype=jnp.int32)
    match = slot_ids[:, None, None] == target[None, :, :]
    filled = jnp.any(match, axis=(1, 2))
    owner = jnp.sum(
        jnp.where(match, jnp.arange(tok_rows, dtype=jnp.int32)[None, :, None], 0), axis=(1, 2)
    )
    send = jnp.where(filled[:, None], hn[owner], jnp.zeros((), jnp.bfloat16)).reshape(
        experts_all, CAP, width
    )
    local_experts = w_gate.shape[0]
    arrived = lax.all_to_all(send, ("ctx", "exp"), split_axis=0, concat_axis=0, tiled=True)
    items = arrived.shape[1]
    sources = arrived.shape[0] // local_experts
    grouped_rows = arrived.reshape(sources, local_experts, items, width)
    gate_v = jnp.einsum("neid,edf->neif", grouped_rows, w_gate, preferred_element_type=jnp.float32)
    up_v = jnp.einsum("neid,edf->neif", grouped_rows, w_up, preferred_element_type=jnp.float32)
    active = (jax.nn.silu(gate_v) * up_v).astype(jnp.bfloat16)
    produced = jnp.einsum(
        "neif,efd->neid", active, w_down, preferred_element_type=jnp.float32
    ).astype(jnp.bfloat16)
    produced = produced.reshape(sources * local_experts, items, width)
    returned = lax.all_to_all(
        produced, ("ctx", "exp"), split_axis=0, concat_axis=0, tiled=True
    ).reshape(experts_all * CAP, width)
    combine = jnp.sum(
        jnp.where(
            slot_ids[None, None, :] == target[:, :, None],
            route_w.astype(jnp.float32)[:, :, None],
            0.0,
        ),
        axis=1,
    ).astype(jnp.bfloat16)
    total_out = jnp.dot(combine, returned, preferred_element_type=jnp.float32) + h1_f
    return total_out.astype(jnp.bfloat16)


def solution(mesh):
    in_specs = (
        P(("ctx", "exp"), None),
        P(("ctx", "exp"), None),
        P(("ctx", "exp"), None),
        P(("ctx", "exp"), None),
        P(),
        P(),
        P(),
        P(("ctx", "exp"), None),
        P(("ctx", "exp"), None, None),
        P(("ctx", "exp"), None, None),
        P(("ctx", "exp"), None, None),
    )
    out_specs = P(("ctx", "exp"), None)
    return jax.shard_map(local, mesh=mesh, in_specs=in_specs, out_specs=out_specs, check_vma=False)
```

profile of v0, /device:TPU:9, one launch (start us, length us, event | category | flops | bytes accessed | tf_op | source)
XLA Modules:
  0.0 637.6 jit_solution(1236187901440541595)
XLA Ops:
  6.5 0.7 all-gather.5.cloned.1.call-update
  7.9 0.9 reshape.224
  9.3 1.5 fusion.51
  10.8 0.8 copy.77
  12.3 0.4 fusion.46
  12.8 0.7 multiply_add_fusion
  13.5 20.5 %fusion.26 = pred[1152]{0:T(1024)(128)(4,1)S(1)} fusion(s32[128,8]{0,1:T(8,128)S(1)} %multiply_add_fusion), kind=kLoop, calls=%fused_computation.37 | loop fusion | flops 2358144 | bytes 5248 | tf_op jit(solution)/shard_map/reduce_or | solution.py:139
  34.3 1.3 copy.86
  35.9 0.3 copy.88
  36.2 20.7 %select_reduce_fusion = s32[1152]{0:T(1024)S(1)} fusion(s32[128,8]{0,1:T(8,128)S(1)} %multiply_add_fusion), kind=kLoop, calls=%fused_computation.35 | loop fusion | flops 3537792 | bytes 8704 | tf_op jit(solution)/shard_map/reduce_sum | solution.py:140
  57.0 10.5 %all-gather.5.cloned.1.call-done = bf16[4096,256]{1,0:T(8,128)(2,1)} async-done(((bf16[128,256]{1,0:T(8,128)(2,1)}), bf16[4096,256]{1,0:T(8,128)(2,1)}) %all-gather.5.cloned.1.call-update) | async-done | bytes 2097168 | tf_op jit(solution)/shard_map/all_gather | solution.py:109
  67.5 4.0 reshape.219
  71.5 54.3 %all-gather.3.cloned.1.call-done = bf16[4096,256]{1,0:T(8,128)(2,1)} async-done(((bf16[128,256]{1,0:T(8,128)(2,1)}), bf16[4096,256]{1,0:T(8,128)(2,1)}) %all-gather.3.cloned.1.call-update) | async-done | bytes 2097168 | tf_op jit(solution)/shard_map/all_gather | solution.py:108
  125.8 4.0 reshape.218
  129.8 42.6 %while.15 = (s32[]{:T(128)}, f32[128,2,8]{0,2,1:T(8,128)S(1)}, f32[128,2,8]{0,2,1:T(8,128)S(1)}, f32[128,2,8,128]{0,3,2,1:T(8,128)}, s32[4]{0:T(128)S(1)}, /*ind...) while((s32[]{:T(128)}, f32[128,2,8]{0,2,1:T(8,128)S(1)}, ...), condition=%wide.region_6.7_spmd.clone, body=%wide.region_3.6_spmd.clone.sunk | while | flops 1101933696 | bytes 41034960 | solution.py:116
  130.2 0.6 dynamic_slice.19
  130.8 0.6 iota_add_fusion.6
  131.6 1.9 constant_dynamic-slice_fusion.3
  133.6 0.4 copy.126
  134.0 1.4 fusion.88
  135.4 2.0 fusion.89
  137.4 2.3 fusion.91
  139.8 1.0 copy-done.3
  140.7 0.6 dynamic_slice.19
  141.3 0.6 iota_add_fusion.6
  142.2 1.9 constant_dynamic-slice_fusion.3
  144.1 0.4 copy.126
  144.5 1.4 fusion.88
  145.9 2.0 fusion.89
  148.0 2.3 fusion.91
  150.3 1.0 copy-done.3
  151.3 0.6 dynamic_slice.19
  151.9 0.6 iota_add_fusion.6
  152.7 1.9 constant_dynamic-slice_fusion.3
  154.7 0.4 copy.126
  155.1 1.4 fusion.88
  156.5 2.0 fusion.89
  158.5 2.3 fusion.91
  160.9 1.0 copy-done.3
  161.8 0.6 dynamic_slice.19
  162.4 0.6 iota_add_fusion.6
  163.3 1.9 constant_dynamic-slice_fusion.3
  165.2 0.4 copy.126
  165.7 1.4 fusion.88
  167.1 2.0 fusion.89
  169.1 2.3 fusion.91
  171.4 1.0 copy-done.3
  172.4 1.3 divide_convert_fusion
  173.8 4.7 multiply_reduce_fusion
  178.7 6.0 gather_fusion
  184.8 8.0 %gather.6 = bf16[128,9,2048]{2,1,0:T(8,128)(2,1)} reshape(bf16[1152,2048]{1,0:T(8,128)(2,1)} %gather_fusion) | data formatting | bytes 9437184 | tf_op jit(solution)/shard_map/gather | solution.py:143
  192.8 7.3 %broadcast_select_fusion = bf16[128,9,2048]{2,1,0:T(8,128)(2,1)} fusion(bf16[128,9,2048]{2,1,0:T(8,128)(2,1)} %gather.6, pred[128,9]{1,0:T(8,128)(4,1)S(1)} %broadcast_in_dim.115), kind=kLoop, calls=%fused_computation.33 | loop fusion | flops 2359296 | bytes 9438336 | tf_op jit(solution)/shard_map/jit(_where)/select_n | solution.py:143
  200.1 186.7 %all_to_all.10 = bf16[128,9,2048]{2,1,0:T(8,128)(2,1)S(1)} all-to-all(bf16[128,9,2048]{2,1,0:T(8,128)(2,1)} %broadcast_select_fusion), channel_id=1, replica_groups=mesh['ctx'=8,'exp'=4] {'ctx','exp'}, dimensions={0} | all-to-all | bytes 9437184 | tf_op jit(solution)/shard_map/all_to_all | solution.py:147
  386.8 3.2 copy-done.1
  390.1 10.0 %fusion.22 = f32[4,32,9,768]{3,1,2,0:T(8,128)} fusion(bf16[4,2048,768]{2,1,0:T(8,128)(2,1)} %param.22, bf16[32,4,9,2048]{3,2,1,0:T(8,128)(2,1)S(1)} %bitcast.129), kind=kOutput, calls=%fused_computation.29 | convolution fusion | flops 3623878656 | bytes 20840448 | tf_op jit(solution)/shard_map/neid,edf->neif/dot_general | solution.py:152
  400.0 18.3 %convert_bitcast_fusion = bf16[32,4,9,2048]{3,0,2,1:T(8,128)(2,1)} fusion(bf16[4,768,2048]{2,1,0:T(8,128)(2,1)} %param.23, f32[4,32,9,768]{3,1,2,0:T(8,128)} %fusion.22, bf16[4,2048,768]{2,1,0:T(8,128)(2,1)} %param.21, bf16[32,4,9,2048]{3,2,1,0:T(8,128)(2,1)} %bitcast.130), kind=kOutput, calls=%fused_computation.34 | convolution fusion | flops 7255425024 | bytes 38141952 | tf_op jit(solution)/shard_map/neif,efd->neid/dot_general | solution.py:154
  418.3 8.6 %copy.106 = bf16[32,4,9,2048]{3,2,1,0:T(8,128)(2,1)} copy(bf16[32,4,9,2048]{3,0,2,1:T(8,128)(2,1)} %convert_bitcast_fusion) | data formatting | bytes 9437184 | tf_op jit(solution)/shard_map/reshape | solution.py:157
  426.9 5.3 all-to-all-start.1
  432.3 0.3 fusion.70
  432.6 0.4 select_reduce_fusion.2
  433.2 1.5 select_reduce_fusion.1
  434.7 183.5 %all-to-all-done.1 = bf16[128,9,2048]{2,1,0:T(8,128)(2,1)} async-done(((bf16[128,9,2048]{2,1,0:T(8,128)(2,1)}), bf16[128,9,2048]{2,1,0:T(8,128)(2,1)}, u32[]{:S(2)}, u32[]{:S(2)}) %all-to-all-start.1) | async-done | bytes 4718624 | tf_op jit(solution)/shard_map/all_to_all | solution.py:158
  618.2 8.4 %reshape.223 = bf16[1152,2048]{1,0:T(8,128)(2,1)} reshape(bf16[128,9,2048]{2,1,0:T(8,128)(2,1)} %all-to-all-done.1) | data formatting | bytes 9437184 | tf_op jit(solution)/shard_map/reshape | solution.py:160
  626.6 4.0 fusion.39
  (80 shorter events, 3.9 us)
Async XLA Ops:
  6.5 425.8 %copy-start = (bf16[2048,128]{1,0:T(8,128)(2,1)S(1)}, bf16[2048,128]{1,0:T(8,128)(2,1)}, u32[]{:S(2)}) copy-start(bf16[2048,128]{1,0:T(8,128)(2,1)} %param.19) | copy-start | bytes 1572868
  6.5 61.0 %all-gather.5.cloned.1.call-start = ((), (), s32[]{:S(2)}) async-start(), calls=%async_computation.3 | async-start | bytes 2162688 | tf_op jit(solution)/shard_map/all_gather | solution.py:109
  7.3 118.5 %all-gather.3.cloned.1.call-start = ((), (), s32[]{:S(2)}) async-start(), calls=%async_computation.2 | async-start | bytes 2162688 | tf_op jit(solution)/shard_map/all_gather | solution.py:108
  129.8 44.0 %copy-start.4 = (bf16[128,2048]{1,0:T(8,128)(2,1)S(1)}, bf16[128,2048]{1,0:T(8,128)(2,1)}, u32[]{:S(2)}) copy-start(bf16[128,2048]{1,0:T(8,128)(2,1)} %param.13) | copy-start | bytes 1572868
  135.3 2.1 copy-start.2
  139.7 1.0 copy-start.3
  145.9 2.1 copy-start.2
  150.3 1.0 copy-start.3
  156.5 2.1 copy-start.2
  160.9 1.0 copy-start.3
  167.0 2.1 copy-start.2
  171.4 1.0 copy-start.3
  173.8 4.8 copy-start.5
  386.8 3.3 copy-start.1
  426.9 191.2 %all-to-all-start.1 = ((bf16[128,9,2048]{2,1,0:T(8,128)(2,1)}), bf16[128,9,2048]{2,1,0:T(8,128)(2,1)}, u32[]{:S(2)}, u32[]{:S(2)}) async-start(bf16[128,9,2048]{2,1,0:T(8,128)(2,1)} %bitcast.126), calls=%async_computation.1 | async-start | bytes 16777216 | tf_op jit(solution)/shard_map/all_to_all | solution.py:158
Sparse Core Ops, SparseCore 0:
  10.3 57.1 all-gather.4
  70.4 55.3 all-gather.2
where the time goes:
time: 648 us; the launch traced here: 638 us
  waiting for transfers between devices  249 us (38%)
  blocking collectives  187 us (29%)
  other arithmetic  67.4 us (10%)
  local copies, waits for them, and re-layouts  62.5 us (10%)
  matrix products  52 us (8%)
  between operations  13.9 us (2%)
    all_to_all x1, blocking collectives, local(): lax.all_to_all(send, ('ctx', 'exp'), split_axis=0, concat_axis=0, tiled=T...  187 us
    all_to_all x1, waiting for transfers between devices, local(): lax.all_to_all(produced, ('ctx', 'exp'), split_axis=0, concat_axis=0, til...  183 us
    all_gather x1, waiting for transfers between devices, local(): key_piece = lax.all_gather(k_flat, ('ctx', 'exp'), axis=0, tiled=True)  54.3 us
    reduce_sum x1, other arithmetic, local(): jnp.sum(jnp.where(match, jnp.arange(tok_rows, dtype=jnp.int32)[None, :, N...  20.7 us
    reduce_or x1, other arithmetic, local(): filled = jnp.any(match, axis=(1, 2))  20.5 us
    dot_general x1, matrix products, local(): jnp.einsum('neif,efd->neid', active, w_down, preferred_element_type=jnp.f...  18.3 us
    gather x2, local copies, waits for them, and re-layouts, local(): hn[owner]  14.1 us
  transfers between devices with their start and end apart: 3, of which 3 were waited for; matrix products, arithmetic and copies ran while one was open for 9% of the time, Pallas kernels for 0%

commit v1 on v0

--- a/solution.py
+++ b/solution.py
@@ -1,12 +1,15 @@
+import functools
 import math
 
 import jax
 import jax.numpy as jnp
+import numpy as np
 from jax import lax
+from jax.experimental import pallas as pl
+from jax.experimental.pallas import tpu as pltpu
 from jax.sharding import PartitionSpec as P
 
 DH = 128
-TOP = 8
 CAP = 9
 
 
@@ -55,6 +58,435 @@
     return (values_f * cos_table[:, None, :] + turned * sin_table[:, None, :]).astype(jnp.bfloat16)
 
 
+def message_rows(sources, own_experts):
+    per = sources * CAP
+    base = per // 16 * 16
+    left = per - base
+    left_rows = -(-(own_experts * left) // 16) * 16
+    total = own_experts * base + left_rows
+    expert = np.zeros(total, np.int32)
+    place = np.zeros(total, np.int32)
+    valid = np.zeros(total, bool)
+    for r in range(total):
+        if r < own_experts * base:
+            expert[r], place[r], valid[r] = r // base, r % base, True
+        elif left and r - own_experts * base < own_experts * left:
+            o = r - own_experts * base
+            expert[r], place[r], valid[r] = o // left, base + o % left, True
+    return base, left, left_rows, total, expert, place // CAP, place % CAP, valid
+
+
+def moe_kernel(
+    sizes,
+    hn_ref,
+    h1_ref,
+    pick_ref,
+    place_ref,
+    chosen_ref,
+    column_expert_ref,
+    router_ref,
+    gate_hbm,
+    up_hbm,
+    down_hbm,
+    out_ref,
+    hall,
+    xs,
+    xr,
+    gate_buf,
+    up_buf,
+    down_buf,
+    acc_g,
+    acc_u,
+    act,
+    yr,
+    left_acc,
+    ps,
+    pr,
+    own_part,
+    combine,
+    wsem,
+    hs_sem,
+    hr_sem,
+    xs_sem,
+    xr_sem,
+    ys_sem,
+    yr_sem,
+    ps_sem,
+    pr_sem,
+):
+    nctx, nexp, epd, tok, base, left, left_rows, rm, chunks, cw = sizes
+    my_c = lax.axis_index("ctx")
+    my_e = lax.axis_index("exp")
+    main = epd * base
+
+    def exp_peer(d):
+        return lax.rem(my_e + d, nexp)
+
+    def ctx_peer(d):
+        return lax.rem(my_c + d, nctx)
+
+    def to_exp(src, dst, ss, rs, peer):
+        return pltpu.make_async_remote_copy(
+            src_ref=src, dst_ref=dst, send_sem=ss, recv_sem=rs,
+            device_id=(my_c, peer), device_id_type=pl.DeviceIdType.MESH,
+        )
+
+    def to_ctx(src, dst, ss, rs, peer):
+        return pltpu.make_async_remote_copy(
+            src_ref=src, dst_ref=dst, send_sem=ss, recv_sem=rs,
+            device_id=(peer, my_e), device_id_type=pl.DeviceIdType.MESH,
+        )
+
+    def weight_copies(k, slot):
+        rows = pl.ds(pl.multiple_of(k * cw, cw), cw)
+        return (
+            pltpu.make_async_copy(gate_hbm.at[:, rows, :], gate_buf.at[slot], wsem.at[0, slot]),
+            pltpu.make_async_copy(up_hbm.at[:, rows, :], up_buf.at[slot], wsem.at[1, slot]),
+        )
+
+    def down_copy(k, slot):
+        columns = pl.ds(pl.multiple_of(k * cw, cw), cw)
+        return pltpu.make_async_copy(
+            down_hbm.at[:, :, columns], down_buf.at[slot], wsem.at[2, slot]
+        )
+
+    barrier = pltpu.get_barrier_semaphore()
+    for d in range(1, nexp):
+        pl.semaphore_signal(
+            barrier, inc=1, device_id=(my_c, exp_peer(d)), device_id_type=pl.DeviceIdType.MESH
+        )
+    for d in range(1, nctx):
+        pl.semaphore_signal(
+            barrier, inc=1, device_id=(ctx_peer(d), my_e), device_id_type=pl.DeviceIdType.MESH
+        )
+    for k in range(2):
+        for copy in weight_copies(k, k):
+            copy.start()
+        down_copy(k, k).start()
+    pl.semaphore_wait(barrier, nexp - 1 + nctx - 1)
+
+    def send_state(k):
+        columns = pl.ds(pl.multiple_of(k * cw, cw), cw)
+
+        def one(d, carry):
+            to_exp(
+                hn_ref.at[:, columns], hall.at[k, my_e], hs_sem.at[k, d], hr_sem.at[k, my_e],
+                exp_peer(d),
+            ).start()
+            return carry
+
+        lax.fori_loop(1, nexp, one, 0)
+        hall[k, my_e] = hn_ref[:, columns]
+
+    def loop(count, body):
+        def step(k, carry):
+            body(k)
+            return carry
+
+        lax.fori_loop(0, count, step, 0)
+
+    loop(chunks, send_state)
+
+    def dispatch(k):
+        def arrived(d, carry):
+            p = exp_peer(d)
+            to_exp(
+                hall.at[k, p], hall.at[k, p], hs_sem.at[k, d], hr_sem.at[k, p], p
+            ).wait_recv()
+            return carry
+
+        lax.fori_loop(1, nexp, arrived, 0)
+        states = hall[k].reshape(nexp * tok, cw)
+
+        def rows_of(c):
+            rows = pl.ds(pl.multiple_of(c * rm, 16), rm)
+            return jnp.dot(
+                pick_ref[rows, :], states, preferred_element_type=jnp.float32
+            ).astype(jnp.bfloat16)
+
+        def one(d, carry):
+            c = ctx_peer(d)
+            xs[k, c] = rows_of(c)
+            to_ctx(xs.at[k, c], xr.at[k, my_c], xs_sem.at[k, d], xr_sem.at[k, my_c], c).start()
+            return carry
+
+        lax.fori_loop(1, nctx, one, 0)
+        xr[k, my_c] = rows_of(my_c)
+
+    loop(chunks, dispatch)
+
+    logits = jnp.zeros((nexp * tok, router_ref.shape[1]), jnp.float32)
+    for k in range(chunks):
+        logits += jnp.dot(
+            hall[k].reshape(nexp * tok, cw),
+            router_ref[k * cw : (k + 1) * cw, :],
+            preferred_element_type=jnp.float32,
+        )
+    raised = jnp.where(chosen_ref[...] > 0.5, jnp.exp(logits), 0.0)
+    route_w = (raised / jnp.sum(raised, axis=-1, keepdims=True)).astype(jnp.bfloat16)
+    combine[...] = (
+        jnp.dot(route_w, column_expert_ref[...], preferred_element_type=jnp.float32).astype(
+            jnp.bfloat16
+        )
+        * place_ref[...]
+    )
+    acc_g[...] = jnp.zeros_like(acc_g)
+    acc_u[...] = jnp.zeros_like(acc_u)
+
+    def enter(k):
+        slot = lax.rem(k, 2)
+
+        def arrived(d, carry):
+            c = ctx_peer(d)
+            to_ctx(xr.at[k, c], xr.at[k, c], xs_sem.at[k, d], xr_sem.at[k, c], c).wait_recv()
+            return carry
+
+        lax.fori_loop(1, nctx, arrived, 0)
+        for copy in weight_copies(k, slot):
+            copy.wait()
+
+        def one(j, carry):
+            front = xr[k, :, pl.ds(pl.multiple_of(j * base, 16), base), :].reshape(nctx * base, cw)
+            gate_w, up_w = gate_buf[slot, j], up_buf[slot, j]
+            top = pl.ds(0, nctx * base)
+            acc_g[j, top, :] += jnp.dot(front, gate_w, preferred_element_type=jnp.float32)
+            acc_u[j, top, :] += jnp.dot(front, up_w, preferred_element_type=jnp.float32)
+            if left_rows:
+                back = xr[k, :, main:rm, :].reshape(nctx * left_rows, cw)
+                low = pl.ds(nctx * base, nctx * left_rows)
+                acc_g[j, low, :] += jnp.dot(back, gate_w, preferred_element_type=jnp.float32)
+                acc_u[j, low, :] += jnp.dot(back, up_w, preferred_element_type=jnp.float32)
+            return carry
+
+        lax.fori_loop(0, epd, one, 0)
+
+        @pl.when(k + 2 < chunks)
+        def _():
+            for copy in weight_copies(k + 2, slot):
+                copy.start()
+
+    loop(chunks, enter)
+
+    def activate(j):
+        g = acc_g[j]
+        act[j] = (g / (1.0 + jnp.exp(-g)) * acc_u[j]).astype(jnp.bfloat16)
+
+    loop(epd, activate)
+
+    def sent_states(k):
+        def one(d, carry):
+            p = exp_peer(d)
+            to_exp(
+                hn_ref.at[:, pl.ds(0, cw)], hall.at[k, my_e], hs_sem.at[k, d], hr_sem.at[k, my_e], p
+            ).wait_send()
+            return carry
+
+        lax.fori_loop(1, nexp, one, 0)
+
+        def two(d, carry):
+            c = ctx_peer(d)
+            to_ctx(
+                xs.at[k, c], xr.at[k, my_c], xs_sem.at[k, d], xr_sem.at[k, my_c], c
+            ).wait_send()
+            return carry
+
+        lax.fori_loop(1, nctx, two, 0)
+
+    loop(chunks, sent_states)
+
+    def leave(k):
+        slot = lax.rem(k, 2)
+        down_copy(k, slot).wait()
+        if left_rows:
+            left_acc[...] = jnp.zeros_like(left_acc)
+
+        def one(j, carry):
+            down_w = down_buf[slot, j]
+            y = jnp.dot(act[j, : nctx * base, :], down_w, preferred_element_type=jnp.float32)
+            xs[k, :, pl.ds(pl.multiple_of(j * base, 16), base), :] = y.astype(
+                jnp.bfloat16
+            ).reshape(nctx, base, cw)
+            if left_rows:
+                y2 = jnp.dot(act[j, nctx * base :, :], down_w, preferred_element_type=jnp.float32)
+                row = lax.broadcasted_iota(jnp.int32, y2.shape, 0) % left_rows
+                mine = (row >= j * left) & (row < (j + 1) * left)
+                left_acc[...] += jnp.where(mine, y2, 0.0)
+            return carry
+
+        lax.fori_loop(0, epd, one, 0)
+        if left_rows:
+            xs[k, :, main:rm, :] = (
+                left_acc[...].astype(jnp.bfloat16).reshape(nctx, left_rows, cw)
+            )
+
+        @pl.when(k + 2 < chunks)
+        def _():
+            down_copy(k + 2, slot).start()
+
+        def push(d, carry):
+            c = ctx_peer(d)
+            to_ctx(xs.at[k, c], yr.at[k, my_c], ys_sem.at[k, d], yr_sem.at[k, my_c], c).start()
+            return carry
+
+        lax.fori_loop(1, nctx, push, 0)
+        yr[k, my_c] = xs[k, my_c]
+
+    loop(chunks, leave)
+
+    def gather_back(k):
+        def arrived(d, carry):
+            c = ctx_peer(d)
+            to_ctx(yr.at[k, c], yr.at[k, c], ys_sem.at[k, d], yr_sem.at[k, c], c).wait_recv()
+            return carry
+
+        lax.fori_loop(1, nctx, arrived, 0)
+        back = yr[k].reshape(nctx * rm, cw)
+
+        def part_of(s):
+            rows = pl.ds(pl.multiple_of(s * tok, tok), tok)
+            return jnp.dot(combine[rows, :], back, preferred_element_type=jnp.float32)
+
+        def one(d, carry):
+            s = exp_peer(d)
+            ps[k, s] = part_of(s).astype(jnp.bfloat16)
+            to_exp(ps.at[k, s], pr.at[k, my_e], ps_sem.at[k, d], pr_sem.at[k, my_e], s).start()
+            return carry
+
+        lax.fori_loop(1, nexp, one, 0)
+        own_part[k] = part_of(my_e)
+
+    loop(chunks, gather_back)
+
+    def finish(k):
+        columns = pl.ds(pl.multiple_of(k * cw, cw), cw)
+        total = h1_ref[:, columns].astype(jnp.float32) + own_part[k]
+
+        def one(d, total):
+            p = exp_peer(d)
+            to_exp(pr.at[k, p], pr.at[k, p], ps_sem.at[k, d], pr_sem.at[k, p], p).wait_recv()
+            return total + pr[k, p].astype(jnp.float32)
+
+        for d in range(1, nexp):
+            total = one(d, total)
+        out_ref[:, columns] = total.astype(jnp.bfloat16)
+
+    loop(chunks, finish)
+
+    def sent_back(k):
+        def one(d, carry):
+            s = exp_peer(d)
+            to_exp(
+                ps.at[k, s], pr.at[k, my_e], ps_sem.at[k, d], pr_sem.at[k, my_e], s
+            ).wait_send()
+            return carry
+
+        lax.fori_loop(1, nexp, one, 0)
+
+        def two(d, carry):
+            c = ctx_peer(d)
+            to_ctx(
+                xs.at[k, c], yr.at[k, my_c], ys_sem.at[k, d], yr_sem.at[k, my_c], c
+            ).wait_send()
+            return carry
+
+        lax.fori_loop(1, nctx, two, 0)
+
+    loop(chunks, sent_back)
+
+
+def expert_part(hn, h1, expert_ids, w_router, w_gate, w_up, w_down):
+    nctx, nexp = lax.axis_size("ctx"), lax.axis_size("exp")
+    my_e = lax.axis_index("exp")
+    tok, width = hn.shape
+    experts_all = w_router.shape[1]
+    epd, _, hidden_units = w_gate.shape
+    base, left, left_rows, rm, row_expert, row_source, row_slot, row_valid = message_rows(nexp, epd)
+    rows_all = nctx * rm
+    ids = lax.all_gather(expert_ids, "exp", axis=0, tiled=False)
+    chosen = jnp.any(
+        ids[:, :, :, None] == jnp.arange(experts_all, dtype=jnp.int32), axis=2
+    )
+    earlier = jnp.asarray(np.tril(np.ones((tok, tok), np.float32), -1), jnp.bfloat16)
+    rank = jnp.einsum(
+        "ut,ste->sue", earlier, chosen.astype(jnp.bfloat16), preferred_element_type=jnp.float32
+    )
+    code = jnp.where(chosen, rank, -1.0).reshape(nexp * tok, experts_all).astype(jnp.bfloat16)
+    row_expert, row_source = np.tile(row_expert, nctx), np.tile(row_source, nctx)
+    row_slot, row_valid = np.tile(row_slot, nctx), np.tile(row_valid, nctx)
+    row_ctx = np.repeat(np.arange(nctx), rm)
+    column_expert_id = jnp.asarray(row_ctx * nexp * epd + row_expert, jnp.int32) + my_e * epd
+    column_expert = (
+        jnp.arange(experts_all, dtype=jnp.int32)[:, None] == column_expert_id[None, :]
+    ).astype(jnp.bfloat16)
+    code_at = jnp.dot(code, column_expert, preferred_element_type=jnp.float32)
+    token_source = np.arange(nexp * tok) // tok
+    place = (
+        (code_at == jnp.asarray(row_slot, jnp.float32)[None, :])
+        & (jnp.asarray(token_source)[:, None] == jnp.asarray(row_source)[None, :])
+        & jnp.asarray(row_valid)[None, :]
+    ).astype(jnp.bfloat16)
+    pick = place.T
+    chunks = 4
+    cw = width // chunks
+    sizes = (nctx, nexp, epd, tok, base, left, left_rows, rm, chunks, cw)
+    mr = nctx * (base + left_rows)
+    bf = jnp.bfloat16
+    vmem = pl.BlockSpec(memory_space=pltpu.VMEM)
+    hbm = pl.BlockSpec(memory_space=pl.ANY)
+    dma = pltpu.SemaphoreType.DMA
+    return pl.pallas_call(
+        functools.partial(moe_kernel, sizes),
+        out_shape=jax.ShapeDtypeStruct((tok, width), bf),
+        in_specs=[vmem] * 7 + [hbm] * 3,
+        out_specs=vmem,
+        scratch_shapes=[
+            pltpu.VMEM((chunks, nexp, tok, cw), bf),
+            pltpu.VMEM((chunks, nctx, rm, cw), bf),
+            pltpu.VMEM((chunks, nctx, rm, cw), bf),
+            pltpu.VMEM((2, epd, cw, hidden_units), bf),
+            pltpu.VMEM((2, epd, cw, hidden_units), bf),
+            pltpu.VMEM((2, epd, hidden_units, cw), bf),
+            pltpu.VMEM((epd, mr, hidden_units), jnp.float32),
+            pltpu.VMEM((epd, mr, hidden_units), jnp.float32),
+            pltpu.VMEM((epd, mr, hidden_units), bf),
+            pltpu.VMEM((chunks, nctx, rm, cw), bf),
+            pltpu.VMEM((nctx * max(left_rows, 16), cw), jnp.float32),
+            pltpu.VMEM((chunks, nexp, tok, cw), bf),
+            pltpu.VMEM((chunks, nexp, tok, cw), bf),
+            pltpu.VMEM((chunks, tok, cw), jnp.float32),
+            pltpu.VMEM((nexp * tok, rows_all), bf),
+            dma((3, 2)),
+            dma((chunks, nexp)),
+            dma((chunks, nexp)),
+            dma((chunks, nctx)),
+            dma((chunks, nctx)),
+            dma((chunks, nctx)),
+            dma((chunks, nctx)),
+            dma((chunks, nexp)),
+            dma((chunks, nexp)),
+        ],
+        compiler_params=pltpu.CompilerParams(
+            collective_id=0, has_side_effects=True, vmem_limit_bytes=63 * 1024 * 1024
+        ),
+        cost_estimate=pl.CostEstimate(
+            flops=6 * epd * mr * width * hidden_units,
+            bytes_accessed=6 * epd * width * hidden_units,
+            transcendentals=0,
+        ),
+    )(
+        hn,
+        h1,
+        pick,
+        place,
+        chosen.reshape(nexp * tok, experts_all).astype(jnp.float32),
+        column_expert,
+        w_router,
+        w_gate,
+        w_up,
+        w_down,
+    )
+
+
 def local(
     hidden, queries, keys, values, w_out, norm_gain, w_router, expert_ids, w_gate, w_up, w_down
 ):
@@ -62,8 +494,6 @@
     kv_heads = keys.shape[1] // DH
     q_heads = queries.shape[1] // DH
     group = q_heads // kv_heads
-    experts_all = w_router.shape[1]
-    width = hidden.shape[1]
     device = lax.axis_index(("ctx", "exp"))
     first_row = device * tok_rows
     positions = first_row + jnp.arange(tok_rows, dtype=jnp.int32)
@@ -124,50 +554,8 @@
         h1_f / jnp.sqrt(jnp.mean(h1_f * h1_f, axis=-1, keepdims=True) + 1e-06) * norm_gain[None, :]
     )
     hn = normed.astype(jnp.bfloat16)
-    logits = jnp.dot(hn, w_router, preferred_element_type=jnp.float32)
-    onehot = expert_ids[:, :, None] == jnp.arange(experts_all, dtype=jnp.int32)[None, None, :]
-    chosen = jnp.sum(jnp.where(onehot, logits[:, None, :], 0.0), axis=-1)
-    raised = jnp.exp(chosen)
-    route_w = (raised / jnp.sum(raised, axis=-1, keepdims=True)).astype(jnp.bfloat16)
-    counts = jnp.cumsum(
-        onehot.reshape(tok_rows * TOP, experts_all).astype(jnp.int32), axis=0
-    ).reshape(tok_rows, TOP, experts_all)
-    slot = jnp.sum(jnp.where(onehot, counts, 0), axis=-1) - 1
-    target = expert_ids * CAP + slot
-    slot_ids = jnp.arange(experts_all * CAP, dtype=jnp.int32)
-    match = slot_ids[:, None, None] == target[None, :, :]
-    filled = jnp.any(match, axis=(1, 2))
-    owner = jnp.sum(
-        jnp.where(match, jnp.arange(tok_rows, dtype=jnp.int32)[None, :, None], 0), axis=(1, 2)
-    )
-    send = jnp.where(filled[:, None], hn[owner], jnp.zeros((), jnp.bfloat16)).reshape(
-        experts_all, CAP, width
-    )
-    local_experts = w_gate.shape[0]
-    arrived = lax.all_to_all(send, ("ctx", "exp"), split_axis=0, concat_axis=0, tiled=True)
-    items = arrived.shape[1]
-    sources = arrived.shape[0] // local_experts
-    grouped_rows = arrived.reshape(sources, local_experts, items, width)
-    gate_v = jnp.einsum("neid,edf->neif", grouped_rows, w_gate, preferred_element_type=jnp.float32)
-    up_v = jnp.einsum("neid,edf->neif", grouped_rows, w_up, preferred_element_type=jnp.float32)
-    active = (jax.nn.silu(gate_v) * up_v).astype(jnp.bfloat16)
-    produced = jnp.einsum(
-        "neif,efd->neid", active, w_down, preferred_element_type=jnp.float32
-    ).astype(jnp.bfloat16)
-    produced = produced.reshape(sources * local_experts, items, width)
-    returned = lax.all_to_all(
-        produced, ("ctx", "exp"), split_axis=0, concat_axis=0, tiled=True
-    ).reshape(experts_all * CAP, width)
-    combine = jnp.sum(
-        jnp.where(
-            slot_ids[None, None, :] == target[:, :, None],
-            route_w.astype(jnp.float32)[:, :, None],
-            0.0,
-        ),
-        axis=1,
-    ).astype(jnp.bfloat16)
-    total_out = jnp.dot(combine, returned, preferred_element_type=jnp.float32) + h1_f
-    return total_out.astype(jnp.bfloat16)
+    mixed = expert_part(hn, h1, expert_ids, w_router, w_gate, w_up, w_down)
+    return mixed
 
 
 def solution(mesh):

time: 648 us -> 368 us (0.57); the launches traced: 638 us -> 366 us
  blocking collectives: 187 us -> 10.8 us
  waiting for transfers between devices: 249 us -> 90.3 us
  Pallas kernels: 0 us -> 147 us
  other arithmetic: 67.4 us -> 31 us
  local copies, waits for them, and re-layouts: 62.5 us -> 26.8 us
    all_to_all x1 -> x0, blocking collectives: 187 us -> none  [local(): lax.all_to_all(send, ('ctx', 'exp'), split_axis=0, concat_axis=0, tiled=T...]
    all_to_all x1 -> x0, waiting for transfers between devices: 183 us -> none  [local(): lax.all_to_all(produced, ('ctx', 'exp'), split_axis=0, concat_axis=0, til...]
    pallas_call x0 -> x1, Pallas kernels: none -> 147 us  [expert_part(): pl.pallas_call(functools.partial(moe_kernel, sizes), out_shape=jax.ShapeD...]
    all_gather x1, waiting for transfers between devices: 10.5 us -> 54.3 us  [local(): value_piece = lax.all_gather(values, ('ctx', 'exp'), axis=0, tiled=True)]
    dot_general x4 -> x2, matrix products: 32.5 us -> 1.03 us  [the longest x1 0.84 us: expert_part(): code_at = jnp.dot(code, column_expert, preferred_element_type=jnp.float32)]
    reduce_sum x5 -> x0, other arithmetic: 23 us -> none  [the longest x1 20.7 us: local(): jnp.sum(jnp.where(match, jnp.arange(tok_rows, dtype=jnp.int32)[None, :, N...]
    all_gather x1, waiting for transfers between devices: 54.3 us -> 35.3 us  [local(): key_piece = lax.all_gather(k_flat, ('ctx', 'exp'), axis=0, tiled=True)]
    reduce_or x1, other arithmetic: 20.5 us -> 2.91 us  [expert_part(): jnp.any(ids[:, :, :, None] == jnp.arange(experts_all, dtype=jnp.int32), a...]
  transfers between devices with their start and end apart: 3 -> 2, of which waited for: 3 -> 2; matrix products, arithmetic and copies ran while one was open for 9% -> 4% of each run, Pallas kernels for 0% -> 0%
where the time goes in v1:
time: 368 us; the launch traced here: 366 us
  Pallas kernels  147 us (40%)
  waiting for transfers between devices  90.3 us (25%)
  matrix products  47 us (13%)
  other arithmetic  31 us (8%)
  local copies, waits for them, and re-layouts  26.8 us (7%)
  between operations  13.7 us (4%)
  blocking collectives  10.8 us (3%)
    pallas_call x1, Pallas kernels, expert_part(): pl.pallas_call(functools.partial(moe_kernel, sizes), out_shape=jax.ShapeD...  147 us
    all_gather x1, waiting for transfers between devices, local(): value_piece = lax.all_gather(values, ('ctx', 'exp'), axis=0, tiled=True)  54.3 us
    all_gather x1, waiting for transfers between devices, local(): key_piece = lax.all_gather(k_flat, ('ctx', 'exp'), axis=0, tiled=True)  35.3 us
    dot_general x4, matrix products, update(): jnp.einsum('thgp,phd->thgd', weights.astype(jnp.bfloat16), value_block, p...  22.9 us
    dot_general x4, matrix products, update(): jnp.einsum('thgd,phd->thgp', q_four, key_block, preferred_element_type=jn...  18.3 us
    reduce_sum x4, other arithmetic, update(): new_sum = run_sum * factor + jnp.sum(weights, axis=-1)  17.8 us
    dynamic_slice x12, local copies, waits for them, and re-layouts, local(): lax.scan(update, initial, (key_blocks, value_blocks, offsets))  11.7 us
    all_gather x1, blocking collectives, expert_part(): ids = lax.all_gather(expert_ids, 'exp', axis=0, tiled=False)  10.8 us
  transfers between devices with their start and end apart: 2, of which 2 were waited for; matrix products, arithmetic and copies ran while one was open for 4% of the time, Pallas kernels for 0%

profile of v1, /device:TPU:9, one launch (start us, length us, event | category | flops | bytes accessed | tf_op | source)
XLA Modules:
  0.0 366.4 jit_solution(17998242440008886149)
XLA Ops:
  6.7 0.2 fusion.35
  7.0 0.1 copy.34
  7.1 0.9 reshape.154
  8.0 0.2 slice_negate_fusion.1
  8.2 0.1 copy.33
  8.3 0.2 maximum_multiply_fusion.1
  8.6 1.5 fusion.32
  10.1 0.7 all-gather.6.cloned.1.call-update
  10.9 1.3 copy.35
  12.3 0.1 slice_negate_fusion
  12.4 0.2 fusion.29
  12.6 0.3 copy.37
  12.8 10.8 %all-gather = s32[512,8]{0,1:T(8,128)S(1)} all-gather(s32[128,8]{0,1:T(8,128)S(1)} %copy-done.5), channel_id=2, replica_groups=mesh['ctx'=8,'exp'=4] {'exp'}, dimensions={0}, use_global_device_ids=true | all-gather | bytes 20480 | tf_op jit(solution)/shard_map/all_gather | solution.py:405
  23.6 0.1 copy.39
  23.8 2.9 fusion.22
  26.7 0.7 convert_element_type.99
  27.4 0.2 fusion.24
  27.6 0.8 fusion.21
  28.5 1.5 copy.40.pick_ref
  30.0 0.8 fusion.30.column_expert_ref
  30.8 1.5 and_convert_fusion.place_ref
  32.3 35.3 %all-gather.4.cloned.1.call-done = bf16[4096,256]{1,0:T(8,128)(2,1)} async-done(((bf16[128,256]{1,0:T(8,128)(2,1)}), bf16[4096,256]{1,0:T(8,128)(2,1)}) %all-gather.4.cloned.1.call-update) | async-done | bytes 2097168 | tf_op jit(solution)/shard_map/all_gather | solution.py:538
  67.5 4.0 %reshape.151 = bf16[4,1024,2,128]{3,2,1,0:T(2,128)(2,1)} reshape(bf16[4096,256]{1,0:T(8,128)(2,1)} %all-gather.4.cloned.1.call-done) | data formatting | bytes 4194304 | tf_op jit(solution)/shard_map/reshape | solution.py:543
  71.5 54.3 %all-gather.6.cloned.1.call-done = bf16[4096,256]{1,0:T(8,128)(2,1)} async-done(((bf16[128,256]{1,0:T(8,128)(2,1)}), bf16[4096,256]{1,0:T(8,128)(2,1)}) %all-gather.6.cloned.1.call-update) | async-done | bytes 2097168 | tf_op jit(solution)/shard_map/all_gather | solution.py:539
  125.8 4.0 %reshape.152 = bf16[4,1024,2,128]{3,2,1,0:T(2,128)(2,1)} reshape(bf16[4096,256]{1,0:T(8,128)(2,1)} %all-gather.6.cloned.1.call-done) | data formatting | bytes 4194304 | tf_op jit(solution)/shard_map/reshape | solution.py:544
  129.8 74.5 %while.15 = (s32[]{:T(128)}, f32[128,2,8]{0,2,1:T(8,128)S(1)}, f32[128,2,8]{0,2,1:T(8,128)S(1)}, f32[128,2,8,128]{0,3,2,1:T(8,128)S(1)}, s32[4]{0:T(128)S(1)}, /...) while((s32[]{:T(128)}, f32[128,2,8]{0,2,1:T(8,128)S(1)}, ...), condition=%wide.region_3.4_spmd.clone, body=%wide.region_0.3_spmd.clone.sunk | while | flops 1101933696 | bytes 32646288 | solution.py:546
  129.8 0.6 dynamic_slice.19
  130.4 0.6 iota_add_fusion.6
  131.1 0.2 broadcast_compare_fusion.2
  131.3 1.9 constant_dynamic-slice_fusion.3
  133.2 4.6 %fusion.64 = (f32[128,2,8]{0,2,1:T(8,128)S(1)}, f32[2,1024,128,8]{2,1,3,0:T(8,128)}) fusion(pred[128,1024]{0,1:T(8,128)(4,1)S(1)} %broadcast_compare_fusion.2, bf16[128,2,8,128]{3,0,2,1:T(8,128)(2,1)S(1)} %get-tuple-element.235, bf16[1,1024,2,128]{3,2,1,0:T(2,128)(2,1)S(1)} %get-tuple-element.201), kind=kOutput, calls=%fused_computation.3.clone.1 | convolution fusion | flops 543160320 | bytes 9576448 | tf_op jit(solution)/shard_map/while/body/eval_jaxpr/thgd,phd->thgp/dot_general | solution.py:515
  137.8 4.5 %fusion.65 = f32[128,2,8]{0,2,1:T(8,128)S(1)} fusion(f32[2,1024,128,8]{2,1,3,0:T(8,128)} %get-tuple-element.203, f32[128,2,8]{0,2,1:T(8,128)S(1)} %select_maximum_fusion.2, pred[128,1024]{0,1:T(8,128)(4,1)S(1)} %broadcast_compare_fusion.2), kind=kLoop, calls=%fused_computation.5.clone.1 | loop fusion | flops 10483712 | bytes 8536064 | tf_op jit(solution)/shard_map/while/body/eval_jaxpr/reduce_sum | solution.py:524
  142.2 0.4 copy.57
  142.7 5.7 %fusion.67 = f32[128,2,8,128]{0,3,2,1:T(8,128)S(1)} fusion(f32[2,1024,128,8]{2,1,3,0:T(8,128)} %get-tuple-element.203, f32[128,2,8]{0,2,1:T(8,128)S(1)} %select_maximum_fusion.2, pred[128,1024]{0,1:T(8,128)(4,1)S(1)} %broadcast_compare_fusion.2, f32[128,2,8,128]{0,3,2,1:T(8,128)S(1)} %get-tuple-element.221, bf16[1,1024,2,128]{1,3,2,0:T(8,128)(2,1)S(1)} %copy.57, ...), kind=kOutput, calls=%fused_computation.9.clone.1 | convolution fusion | flops 548143104 | bytes 11157505 | tf_op jit(solution)/shard_map/while/body/eval_jaxpr/thgp,phd->thgd/dot_general | solution.py:525
  148.4 0.6 dynamic_slice.19
  149.0 0.6 iota_add_fusion.6
  149.7 0.2 broadcast_compare_fusion.2
  149.9 1.9 constant_dynamic-slice_fusion.3
  151.8 4.6 %fusion.64 = (f32[128,2,8]{0,2,1:T(8,128)S(1)}, f32[2,1024,128,8]{2,1,3,0:T(8,128)}) fusion(pred[128,1024]{0,1:T(8,128)(4,1)S(1)} %broadcast_compare_fusion.2, bf16[128,2,8,128]{3,0,2,1:T(8,128)(2,1)S(1)} %get-tuple-element.235, bf16[1,1024,2,128]{3,2,1,0:T(2,128)(2,1)S(1)} %get-tuple-element.201), kind=kOutput, calls=%fused_computation.3.clone.1 | convolution fusion | flops 543160320 | bytes 9576448 | tf_op jit(solution)/shard_map/while/body/eval_jaxpr/thgd,phd->thgp/dot_general | solution.py:515
  156.4 4.5 %fusion.65 = f32[128,2,8]{0,2,1:T(8,128)S(1)} fusion(f32[2,1024,128,8]{2,1,3,0:T(8,128)} %get-tuple-element.203, f32[128,2,8]{0,2,1:T(8,128)S(1)} %select_maximum_fusion.2, pred[128,1024]{0,1:T(8,128)(4,1)S(1)} %broadcast_compare_fusion.2), kind=kLoop, calls=%fused_computation.5.clone.1 | loop fusion | flops 10483712 | bytes 8536064 | tf_op jit(solution)/shard_map/while/body/eval_jaxpr/reduce_sum | solution.py:524
  160.9 0.4 copy.57
  161.3 5.7 %fusion.67 = f32[128,2,8,128]{0,3,2,1:T(8,128)S(1)} fusion(f32[2,1024,128,8]{2,1,3,0:T(8,128)} %get-tuple-element.203, f32[128,2,8]{0,2,1:T(8,128)S(1)} %select_maximum_fusion.2, pred[128,1024]{0,1:T(8,128)(4,1)S(1)} %broadcast_compare_fusion.2, f32[128,2,8,128]{0,3,2,1:T(8,128)S(1)} %get-tuple-element.221, bf16[1,1024,2,128]{1,3,2,0:T(8,128)(2,1)S(1)} %copy.57, ...), kind=kOutput, calls=%fused_computation.9.clone.1 | convolution fusion | flops 548143104 | bytes 11157505 | tf_op jit(solution)/shard_map/while/body/eval_jaxpr/thgp,phd->thgd/dot_general | solution.py:525
  167.1 0.6 dynamic_slice.19
  167.7 0.6 iota_add_fusion.6
  168.3 0.2 broadcast_compare_fusion.2
  168.5 1.9 constant_dynamic-slice_fusion.3
  170.5 4.6 %fusion.64 = (f32[128,2,8]{0,2,1:T(8,128)S(1)}, f32[2,1024,128,8]{2,1,3,0:T(8,128)}) fusion(pred[128,1024]{0,1:T(8,128)(4,1)S(1)} %broadcast_compare_fusion.2, bf16[128,2,8,128]{3,0,2,1:T(8,128)(2,1)S(1)} %get-tuple-element.235, bf16[1,1024,2,128]{3,2,1,0:T(2,128)(2,1)S(1)} %get-tuple-element.201), kind=kOutput, calls=%fused_computation.3.clone.1 | convolution fusion | flops 543160320 | bytes 9576448 | tf_op jit(solution)/shard_map/while/body/eval_jaxpr/thgd,phd->thgp/dot_general | solution.py:515
  175.0 4.5 %fusion.65 = f32[128,2,8]{0,2,1:T(8,128)S(1)} fusion(f32[2,1024,128,8]{2,1,3,0:T(8,128)} %get-tuple-element.203, f32[128,2,8]{0,2,1:T(8,128)S(1)} %select_maximum_fusion.2, pred[128,1024]{0,1:T(8,128)(4,1)S(1)} %broadcast_compare_fusion.2), kind=kLoop, calls=%fused_computation.5.clone.1 | loop fusion | flops 10483712 | bytes 8536064 | tf_op jit(solution)/shard_map/while/body/eval_jaxpr/reduce_sum | solution.py:524
  179.5 0.4 copy.57
  179.9 5.7 %fusion.67 = f32[128,2,8,128]{0,3,2,1:T(8,128)S(1)} fusion(f32[2,1024,128,8]{2,1,3,0:T(8,128)} %get-tuple-element.203, f32[128,2,8]{0,2,1:T(8,128)S(1)} %select_maximum_fusion.2, pred[128,1024]{0,1:T(8,128)(4,1)S(1)} %broadcast_compare_fusion.2, f32[128,2,8,128]{0,3,2,1:T(8,128)S(1)} %get-tuple-element.221, bf16[1,1024,2,128]{1,3,2,0:T(8,128)(2,1)S(1)} %copy.57, ...), kind=kOutput, calls=%fused_computation.9.clone.1 | convolution fusion | flops 548143104 | bytes 11157505 | tf_op jit(solution)/shard_map/while/body/eval_jaxpr/thgp,phd->thgd/dot_general | solution.py:525
  185.7 0.6 dynamic_slice.19
  186.3 0.6 iota_add_fusion.6
  187.0 0.2 broadcast_compare_fusion.2
  187.2 1.9 constant_dynamic-slice_fusion.3
  189.1 4.6 %fusion.64 = (f32[128,2,8]{0,2,1:T(8,128)S(1)}, f32[2,1024,128,8]{2,1,3,0:T(8,128)}) fusion(pred[128,1024]{0,1:T(8,128)(4,1)S(1)} %broadcast_compare_fusion.2, bf16[128,2,8,128]{3,0,2,1:T(8,128)(2,1)S(1)} %get-tuple-element.235, bf16[1,1024,2,128]{3,2,1,0:T(2,128)(2,1)S(1)} %get-tuple-element.201), kind=kOutput, calls=%fused_computation.3.clone.1 | convolution fusion | flops 543160320 | bytes 9576448 | tf_op jit(solution)/shard_map/while/body/eval_jaxpr/thgd,phd->thgp/dot_general | solution.py:515
  193.7 4.5 %fusion.65 = f32[128,2,8]{0,2,1:T(8,128)S(1)} fusion(f32[2,1024,128,8]{2,1,3,0:T(8,128)} %get-tuple-element.203, f32[128,2,8]{0,2,1:T(8,128)S(1)} %select_maximum_fusion.2, pred[128,1024]{0,1:T(8,128)(4,1)S(1)} %broadcast_compare_fusion.2), kind=kLoop, calls=%fused_computation.5.clone.1 | loop fusion | flops 10483712 | bytes 8536064 | tf_op jit(solution)/shard_map/while/body/eval_jaxpr/reduce_sum | solution.py:524
  198.2 0.4 copy.57
  198.6 5.7 %fusion.67 = f32[128,2,8,128]{0,3,2,1:T(8,128)S(1)} fusion(f32[2,1024,128,8]{2,1,3,0:T(8,128)} %get-tuple-element.203, f32[128,2,8]{0,2,1:T(8,128)S(1)} %select_maximum_fusion.2, pred[128,1024]{0,1:T(8,128)(4,1)S(1)} %broadcast_compare_fusion.2, f32[128,2,8,128]{0,3,2,1:T(8,128)S(1)} %get-tuple-element.221, bf16[1,1024,2,128]{1,3,2,0:T(8,128)(2,1)S(1)} %copy.57, ...), kind=kOutput, calls=%fused_computation.9.clone.1 | convolution fusion | flops 548143104 | bytes 11157505 | tf_op jit(solution)/shard_map/while/body/eval_jaxpr/thgp,phd->thgd/dot_general | solution.py:525
  204.3 0.1 divide_convert_fusion
  204.5 4.8 %fusion.25 = (f32[128]{0:T(128)S(1)}, bf16[128,2048]{1,0:T(8,128)(2,1)S(1)}) fusion(bf16[128,2048]{1,0:T(8,128)(2,1)S(1)} %copy-done.1, bf16[128,2048]{0,1:T(8,128)(2,1)S(1)} %bitcast.87, bf16[2048,2048]{1,0:T(8,128)(2,1)} %param.23), kind=kOutput, calls=%fused_computation.39 | convolution fusion | flops 1075314560 | bytes 9961984 | tf_op jit(solution)/shard_map/dot_general | solution.py:550
  209.3 0.8 copy-done
  210.1 1.0 fusion.27.hn_ref
  211.1 146.6 %shard_map.163 = bf16[128,2048]{1,0:T(8,128)(2,1)} custom-call(bf16[128,2048]{1,0:T(8,128)(2,1)} %fusion.27.hn_ref, bf16[128,2048]{1,0:T(8,128)(2,1)} %copy-done, bf16[1152,512]{1,0:T(8,128)(2,1)} %copy.40.pick_ref, bf16[512,1152]{1,0:T(8,128)(2,1)} %and_convert_fusion.place_ref, f32[512,128]{1,0:T(8,128)} %bitcast.92, ...), custom_call_target="tpu_custom_call" | custom-call | flops 14495514624 | bytes 37748736 | tf_op jit(solution)/shard_map/pallas_call | solution.py:437
  357.7 1.9 copy.71
  (47 shorter events, 0.5 us)
Async XLA Ops:
  6.5 20.9 %copy-start.4 = (s32[1152]{0:T(1024)S(1)}, s32[1152]{0:T(1024)}, u32[]{:S(2)}) copy-start(s32[1152]{0:T(1024)} %constant.81.clone) | copy-start | bytes 13828
  6.5 20.9 %copy-start.7 = (bf16[128,128,1]{1,0,2:T(8,128)(2,1)S(1)}, bf16[128,128,1]{1,0,2:T(8,128)(2,1)}, u32[]{:S(2)}) copy-start(bf16[128,128,1]{1,0,2:T(8,128)(2,1)} %constant.89) | copy-start | bytes 98308
  6.5 21.1 %copy-start.8 = (f32[1152]{0:T(1024)S(1)}, f32[1152]{0:T(1024)}, u32[]{:S(2)}) copy-start(f32[1152]{0:T(1024)} %constant.82.clone) | copy-start | bytes 13828
  6.5 21.1 %copy-start.6 = (s32[512]{0:T(512)S(1)}, s32[512]{0:T(512)}, u32[]{:S(2)}) copy-start(s32[512]{0:T(512)} %constant.83.clone) | copy-start | bytes 6148
  6.5 21.1 %copy-start.3 = (s32[1152]{0:T(1024)S(1)}, s32[1152]{0:T(1024)}, u32[]{:S(2)}) copy-start(s32[1152]{0:T(1024)} %constant.84.clone) | copy-start | bytes 13828
  6.6 6.3 %copy-start.5 = (s32[128,8]{0,1:T(8,128)S(1)}, s32[128,8]{0,1:T(8,128)}, u32[]{:S(2)}) copy-start(s32[128,8]{0,1:T(8,128)} %param.26) | copy-start | bytes 12292
  6.6 61.0 %all-gather.4.cloned.1.call-start = ((), (), s32[]{:S(2)}) async-start(), calls=%async_computation | async-start | bytes 2162688 | tf_op jit(solution)/shard_map/all_gather | solution.py:538
  10.1 115.7 %all-gather.6.cloned.1.call-start = ((), (), s32[]{:S(2)}) async-start(), calls=%async_computation.1 | async-start | bytes 2162688 | tf_op jit(solution)/shard_map/all_gather | solution.py:539
  129.8 74.7 %copy-start.1 = (bf16[128,2048]{1,0:T(8,128)(2,1)S(1)}, bf16[128,2048]{1,0:T(8,128)(2,1)}, u32[]{:S(2)}) copy-start(bf16[128,2048]{1,0:T(8,128)(2,1)} %param.19) | copy-start | bytes 1572868
  204.5 5.6 %copy-start.2 = (f32[2048]{0:T(1024)S(1)}, f32[2048]{0:T(1024)}, u32[]{:S(2)}) copy-start(f32[2048]{0:T(1024)} %param.24) | copy-start | bytes 24580
  209.3 0.8 copy-start
Sparse Core Ops, SparseCore 0:
  10.3 57.1 all-gather.3
  70.5 55.3 all-gather.5

commit v2 on v1

--- a/solution.py
+++ b/solution.py
@@ -394,7 +394,7 @@
     loop(chunks, sent_back)
 
 
-def expert_part(hn, h1, expert_ids, w_router, w_gate, w_up, w_down):
+def expert_part(hn, h1, ids, w_router, w_gate, w_up, w_down):
     nctx, nexp = lax.axis_size("ctx"), lax.axis_size("exp")
     my_e = lax.axis_index("exp")
     tok, width = hn.shape
@@ -402,7 +402,6 @@
     epd, _, hidden_units = w_gate.shape
     base, left, left_rows, rm, row_expert, row_source, row_slot, row_valid = message_rows(nexp, epd)
     rows_all = nctx * rm
-    ids = lax.all_gather(expert_ids, "exp", axis=0, tiled=False)
     chosen = jnp.any(
         ids[:, :, :, None] == jnp.arange(experts_all, dtype=jnp.int32), axis=2
     )
@@ -487,6 +486,253 @@
     )
 
 
+def attend_kernel(
+    sizes,
+    q_ref,
+    kv_ref,
+    ids_ref,
+    out_ref,
+    ids_out,
+    kv,
+    ids_all,
+    peak,
+    total,
+    acc,
+    is_sem,
+    ir_sem,
+    zs_sem,
+    zr_sem,
+    xs_sem,
+    xr_sem,
+    fs_sem,
+    fr_sem,
+):
+    nctx, nexp, tok, kv_heads, group = sizes
+    my_c, my_e = lax.axis_index("ctx"), lax.axis_index("exp")
+    pairs = nctx // 2
+    my_h, core = my_c // 2, lax.rem(my_c, 2)
+    partner = my_h * 2 + 1 - core
+    mesh_id = pl.DeviceIdType.MESH
+
+    def exp_peer(d):
+        return lax.rem(my_e + d, nexp)
+
+    def pair_peer(d):
+        return lax.rem(my_h + d, pairs)
+
+    def copy_to(src, dst, ss, rs, c, e):
+        return pltpu.make_async_remote_copy(
+            src_ref=src, dst_ref=dst, send_sem=ss, recv_sem=rs,
+            device_id=(c, e), device_id_type=mesh_id,
+        )
+
+    def to_exp(d):
+        return copy_to(
+            kv_ref, kv.at[my_c, my_e], zs_sem.at[d], zr_sem.at[my_e], my_c, exp_peer(d)
+        )
+
+    def ids_to(d):
+        return copy_to(
+            ids_ref, ids_all.at[my_e], is_sem.at[d], ir_sem.at[my_e], my_c, exp_peer(d)
+        )
+
+    def to_pair(s, d):
+        return copy_to(
+            kv.at[my_c, s], kv.at[my_c, s], xs_sem.at[s, d], xr_sem.at[s, my_h],
+            pair_peer(d) * 2 + core, my_e,
+        )
+
+    def to_partner(s, h):
+        c = h * 2 + core
+        return copy_to(
+            kv.at[c, s], kv.at[c, s], fs_sem.at[s, h], fr_sem.at[s, h], partner, my_e
+        )
+
+    barrier = pltpu.get_barrier_semaphore()
+    for d in range(1, nexp):
+        pl.semaphore_signal(
+            barrier, inc=1, device_id=(my_c, exp_peer(d)), device_id_type=mesh_id
+        )
+    for d in range(1, pairs):
+        pl.semaphore_signal(
+            barrier, inc=1, device_id=(pair_peer(d) * 2 + core, my_e), device_id_type=mesh_id
+        )
+    pl.semaphore_signal(barrier, inc=1, device_id=(partner, my_e), device_id_type=mesh_id)
+    kv[my_c, my_e] = kv_ref[...]
+    ids_all[my_e] = ids_ref[...]
+    pl.semaphore_wait(barrier, nexp - 1 + pairs - 1 + 1)
+
+    def loop(low, high, body):
+        def step(i, carry):
+            body(i)
+            return carry
+
+        lax.fori_loop(low, high, step, 0)
+
+    loop(1, nexp, lambda d: to_exp(d).start())
+    loop(1, nexp, lambda d: ids_to(d).start())
+
+    def spread(s):
+        loop(1, pairs, lambda d: to_pair(s, d).start())
+        to_partner(s, my_h).start()
+
+    spread(my_e)
+
+    def from_exp(d):
+        s = exp_peer(d)
+        copy_to(
+            kv.at[my_c, s], kv.at[my_c, s], zs_sem.at[d], zr_sem.at[s], my_c, s
+        ).wait_recv()
+        spread(s)
+
+    loop(1, nexp, from_exp)
+
+    factor = (1.0 / math.sqrt(DH)) * math.log2(math.e)
+    span = nexp * tok
+    heads = 2 if group % 2 == 0 else 1
+    rows = heads * tok
+
+    def block(c, first):
+        def one(i, carry):
+            at = pl.ds(pl.multiple_of(i * rows, rows), rows)
+            q = q_ref[at, :]
+            g = i * heads // group
+            head_cols = pl.ds(pl.multiple_of(g * DH, DH), DH)
+            value_cols = pl.ds(pl.multiple_of((kv_heads + g) * DH, DH), DH)
+            k = kv[c, :, :, head_cols].reshape(span, DH)
+            v = kv[c, :, :, value_cols].reshape(span, DH)
+            scores = lax.dot_general(
+                q, k, (((1,), (1,)), ((), ())), preferred_element_type=jnp.float32
+            ) * factor
+            if first:
+                t = lax.broadcasted_iota(jnp.int32, scores.shape, 0) % tok
+                u = lax.broadcasted_iota(jnp.int32, scores.shape, 1)
+                scores = jnp.where(u <= t + my_e * tok, scores, -1e30)
+                top = jnp.max(scores, axis=-1, keepdims=True)
+                w = jnp.exp2(scores - top)
+                total[at, :] = jnp.broadcast_to(jnp.sum(w, axis=-1, keepdims=True), (rows, DH))
+                peak[at, :] = jnp.broadcast_to(top, (rows, DH))
+                acc[at, :] = jnp.dot(
+                    w.astype(jnp.bfloat16), v, preferred_element_type=jnp.float32
+                )
+            else:
+                old = peak[at, :]
+                new = jnp.maximum(old, jnp.max(scores, axis=-1, keepdims=True))
+                w = jnp.exp2(scores - new[:, :1])
+                fade = jnp.exp2(old - new)
+                total[at, :] = total[at, :] * fade + jnp.sum(w, axis=-1, keepdims=True)
+                peak[at, :] = new
+                acc[at, :] = acc[at, :] * fade + jnp.dot(
+                    w.astype(jnp.bfloat16), v, preferred_element_type=jnp.float32
+                )
+            return carry
+
+        lax.fori_loop(0, kv_heads * group // heads, one, 0)
+
+    block(my_c, True)
+
+    def forward(s):
+        def one(d):
+            h = pair_peer(d)
+            c = h * 2 + core
+            copy_to(
+                kv.at[c, s], kv.at[c, s], xs_sem.at[s, d], xr_sem.at[s, h], c, my_e
+            ).wait_recv()
+            to_partner(s, h).start()
+
+        loop(1, pairs, one)
+
+    loop(0, nexp, forward)
+
+    def same_core(d):
+        c = pair_peer(d) * 2 + core
+
+        @pl.when(c < my_c)
+        def _():
+            block(c, False)
+
+    loop(1, pairs, same_core)
+
+    def other_core(d):
+        h = pair_peer(d)
+        c = h * 2 + 1 - core
+
+        def arrived(s):
+            copy_to(
+                kv.at[c, s], kv.at[c, s], fs_sem.at[s, h], fr_sem.at[s, h], partner, my_e
+            ).wait_recv()
+
+        loop(0, nexp, arrived)
+
+        @pl.when(c < my_c)
+        def _():
+            block(c, False)
+
+    loop(0, pairs, other_core)
+
+    for i in range(kv_heads * group):
+        at = slice(i * tok, (i + 1) * tok)
+        out_ref[:, i * DH : (i + 1) * DH] = (acc[at, :] / total[at, :]).astype(jnp.bfloat16)
+
+    def from_ids(d):
+        s = exp_peer(d)
+        copy_to(
+            ids_all.at[s], ids_all.at[s], is_sem.at[d], ir_sem.at[s], my_c, s
+        ).wait_recv()
+
+    loop(1, nexp, from_ids)
+    ids_out[...] = ids_all[...]
+
+    def sent(s):
+        loop(1, pairs, lambda d: to_pair(s, d).wait_send())
+        loop(0, pairs, lambda h: to_partner(s, h).wait_send())
+
+    loop(0, nexp, sent)
+    loop(1, nexp, lambda d: to_exp(d).wait_send())
+    loop(1, nexp, lambda d: ids_to(d).wait_send())
+
+
+def attend(q, kv, expert_ids, kv_heads, group):
+    nctx, nexp = lax.axis_size("ctx"), lax.axis_size("exp")
+    tok, width = kv.shape
+    bf = jnp.bfloat16
+    rows = q.shape[0]
+    vmem = pl.BlockSpec(memory_space=pltpu.VMEM)
+    dma = pltpu.SemaphoreType.DMA
+    return pl.pallas_call(
+        functools.partial(attend_kernel, (nctx, nexp, tok, kv_heads, group)),
+        out_shape=(
+            jax.ShapeDtypeStruct((tok, kv_heads * group * DH), bf),
+            jax.ShapeDtypeStruct((nexp,) + expert_ids.shape, jnp.int32),
+        ),
+        in_specs=[vmem] * 3,
+        out_specs=(vmem, vmem),
+        scratch_shapes=[
+            pltpu.VMEM((nctx, nexp, tok, width), bf),
+            pltpu.VMEM((nexp,) + expert_ids.shape, jnp.int32),
+            pltpu.VMEM((rows, DH), jnp.float32),
+            pltpu.VMEM((rows, DH), jnp.float32),
+            pltpu.VMEM((rows, DH), jnp.float32),
+            dma((nexp,)),
+            dma((nexp,)),
+            dma((nexp,)),
+            dma((nexp,)),
+            dma((nexp, nctx // 2)),
+            dma((nexp, nctx // 2)),
+            dma((nexp, nctx // 2)),
+            dma((nexp, nctx // 2)),
+        ],
+        compiler_params=pltpu.CompilerParams(
+            collective_id=1, has_side_effects=True, vmem_limit_bytes=48 * 1024 * 1024
+        ),
+        cost_estimate=pl.CostEstimate(
+            flops=4 * rows * nctx * nexp * tok * DH,
+            bytes_accessed=nctx * nexp * tok * width * 2,
+            transcendentals=rows * nctx * nexp * tok,
+        ),
+    )(q, kv, expert_ids)
+
+
 def local(
     hidden, queries, keys, values, w_out, norm_gain, w_router, expert_ids, w_gate, w_up, w_down
 ):
@@ -498,54 +744,15 @@
     first_row = device * tok_rows
     positions = first_row + jnp.arange(tok_rows, dtype=jnp.int32)
     cos_table, sin_table = yarn_tables(positions, DH)
-    q_four = rotate(queries.reshape(tok_rows, q_heads, DH), cos_table, sin_table).reshape(
-        tok_rows, kv_heads, group, DH
-    )
+    q_rows = jnp.swapaxes(
+        rotate(queries.reshape(tok_rows, q_heads, DH), cos_table, sin_table), 0, 1
+    ).reshape(q_heads * tok_rows, DH)
     k_flat = rotate(keys.reshape(tok_rows, kv_heads, DH), cos_table, sin_table).reshape(
         tok_rows, kv_heads * DH
     )
-    q_rows = first_row + jnp.arange(tok_rows, dtype=jnp.int32)
-    scale = 1.0 / math.sqrt(DH)
-
-    def update(carry, operands):
-        run_max, run_sum, run_acc = carry
-        key_block, value_block, block_start = operands
-        block_len = key_block.shape[0]
-        scores = (
-            jnp.einsum("thgd,phd->thgp", q_four, key_block, preferred_element_type=jnp.float32)
-            * scale
-        )
-        key_rows = block_start + jnp.arange(block_len, dtype=jnp.int32)
-        allowed = (key_rows[None, :] <= q_rows[:, None])[:, None, None, :]
-        scores = jnp.where(allowed, scores, -1e30)
-        new_max = jnp.maximum(run_max, jnp.max(scores, axis=-1))
-        weights = jnp.where(allowed, jnp.exp(scores - new_max[..., None]), 0.0)
-        factor = jnp.exp(run_max - new_max)
-        new_sum = run_sum * factor + jnp.sum(weights, axis=-1)
-        added = jnp.einsum(
-            "thgp,phd->thgd",
-            weights.astype(jnp.bfloat16),
-            value_block,
-            preferred_element_type=jnp.float32,
-        )
-        return ((new_max, new_sum, run_acc * factor[..., None] + added), None)
-
-    initial = (
-        jnp.full((tok_rows, kv_heads, group), -1e30, jnp.float32),
-        jnp.zeros((tok_rows, kv_heads, group), jnp.float32),
-        jnp.zeros((tok_rows, kv_heads, group, DH), jnp.float32),
-    )
-    key_piece = lax.all_gather(k_flat, ("ctx", "exp"), axis=0, tiled=True)
-    value_piece = lax.all_gather(values, ("ctx", "exp"), axis=0, tiled=True)
-    piece_len = key_piece.shape[0]
-    block_len = math.gcd(piece_len, 1024)
-    count = piece_len // block_len
-    key_blocks = key_piece.reshape(count, block_len, kv_heads, DH)
-    value_blocks = value_piece.reshape(count, block_len, kv_heads, DH)
-    offsets = jnp.arange(count, dtype=jnp.int32) * block_len
-    result, unused = lax.scan(update, initial, (key_blocks, value_blocks, offsets))
-    final_max, final_sum, final_acc = result
-    attn = (final_acc / final_sum[..., None]).astype(jnp.bfloat16).reshape(tok_rows, q_heads * DH)
+    attn, ids = attend(
+        q_rows, jnp.concatenate([k_flat, values], axis=1), expert_ids, kv_heads, group
+    )
     h1 = (
         jnp.dot(attn, w_out, preferred_element_type=jnp.float32) + hidden.astype(jnp.float32)
     ).astype(jnp.bfloat16)
@@ -554,7 +761,7 @@
         h1_f / jnp.sqrt(jnp.mean(h1_f * h1_f, axis=-1, keepdims=True) + 1e-06) * norm_gain[None, :]
     )
     hn = normed.astype(jnp.bfloat16)
-    mixed = expert_part(hn, h1, expert_ids, w_router, w_gate, w_up, w_down)
+    mixed = expert_part(hn, h1, ids, w_router, w_gate, w_up, w_down)
     return mixed
 
 

time: 368 us -> 236 us (0.64)
  waiting for transfers between devices: 90.3 us -> 0 us
  Pallas kernels: 147 us -> 216 us
  matrix products: 47 us -> 5.85 us
  local copies, waits for them, and re-layouts: 26.8 us -> 3.83 us
  other arithmetic: 31 us -> 9.7 us
  between operations: 13.7 us -> 0.31 us
  blocking collectives: 10.8 us -> 0 us
    all_gather x2 -> x0, waiting for transfers between devices: 89.6 us -> none  [the longest x1 54.3 us: local(): value_piece = lax.all_gather(values, ('ctx', 'exp'), axis=0, tiled=True)]
    dot_general x8 -> x0, matrix products: 41.2 us -> none  [the longest x4 22.9 us: update(): jnp.einsum('thgp,phd->thgd', weights.astype(jnp.bfloat16), value_block, p...]
    pallas_call x0 -> x1, Pallas kernels: none -> 40.6 us  [attend(): pl.pallas_call(functools.partial(attend_kernel, (nctx, nexp, tok, kv_head...]
    pallas_call x1, Pallas kernels: 147 us -> 175 us  [expert_part(): pl.pallas_call(functools.partial(moe_kernel, sizes), out_shape=jax.ShapeD...]
    reduce_sum x4 -> x0, other arithmetic: 17.8 us -> none  [update(): new_sum = run_sum * factor + jnp.sum(weights, axis=-1)]
    dynamic_slice x12 -> x0, local copies, waits for them, and re-layouts: 11.7 us -> none  [local(): lax.scan(update, initial, (key_blocks, value_blocks, offsets))]
    all_gather x1 -> x0, blocking collectives: 10.8 us -> none  [expert_part(): ids = lax.all_gather(expert_ids, 'exp', axis=0, tiled=False)]
    reshape x2 -> x0, local copies, waits for them, and re-layouts: 7.97 us -> none  [the longest x1 4 us: local(): key_blocks = key_piece.reshape(count, block_len, kv_heads, DH)]
  transfers between devices with their start and end apart: 2 -> 0, of which waited for: 2 -> 0; matrix products, arithmetic and copies ran while one was open for 4% -> 0% of each run, Pallas kernels for 0% -> 0%
where the time goes in v2:
time: 236 us
  Pallas kernels  216 us (92%)
  other arithmetic  9.7 us (4%)
  matrix products  5.85 us (2%)
  local copies, waits for them, and re-layouts  3.83 us (2%)
    pallas_call x1, Pallas kernels, expert_part(): pl.pallas_call(functools.partial(moe_kernel, sizes), out_shape=jax.ShapeD...  175 us
    pallas_call x1, Pallas kernels, attend(): pl.pallas_call(functools.partial(attend_kernel, (nctx, nexp, tok, kv_head...  40.6 us
    dot_general x1, matrix products, local(): jnp.dot(attn, w_out, preferred_element_type=jnp.float32)  4.83 us

profile of v2, /device:TPU:9, one launch (start us, length us, event | category | flops | bytes accessed | tf_op | source)
XLA Modules:
  0.0 235.7 jit_solution(6801466626615565869)
XLA Ops:
  0.0 1.1 copy_bitcast_fusion
  1.1 0.0 copy-start
  1.2 0.4 slice_negate_fusion
  1.5 0.0 copy-start.3
  1.6 0.1 broadcast_multiply_fusion
  1.7 0.3 cosine_multiply_fusion
  2.0 0.2 copy-done
  2.2 0.0 copy-start.4
  2.2 0.0 copy-start.8
  2.2 0.4 fusion.9
  2.6 0.0 copy-done.3
  2.6 0.1 reshape.111
  2.7 0.2 slice_negate_fusion.1
  2.9 0.2 maximum_multiply_fusion.1
  3.2 0.0 copy-done.4
  3.2 0.0 copy-done.8
  3.2 0.1 copy.26.ids_ref
  3.3 0.0 copy-start.2
  3.3 40.6 %shard_map.163 = (bf16[128,2048]{1,0:T(8,128)(2,1)S(1)}, s32[4,128,8]{2,1,0:T(8,128)S(1)}) custom-call(bf16[2048,128]{1,0:T(8,128)(2,1)S(1)} %bitcast.39, bf16[128,512]{1,0:T(8,128)(2,1)S(1)} %pad_maximum_fusion.kv_ref, s32[128,8]{1,0:T(8,128)S(1)} %copy.26.ids_ref), custom_call_target="tpu_custom_call" | custom-call | flops 4294967296 | bytes 4194304 | tf_op jit(solution)/shard_map/pallas_call | solution.py:702
  43.9 0.0 copy-done.2
  43.9 0.0 copy-start.5
  44.0 0.0 copy-start.10
  44.0 0.0 copy-start.7
  44.0 0.0 copy-start.6
  44.0 0.0 copy-start.9
  44.0 0.0 copy-start.11
  44.0 4.8 %fusion.5 = (f32[128]{0:T(128)S(1)}, bf16[128,2048]{1,0:T(8,128)(2,1)S(1)}) fusion(bf16[128,2048]{1,0:T(8,128)(2,1)S(1)} %copy-done.2, bf16[128,2048]{1,0:T(8,128)(2,1)S(1)} %get-tuple-element.7, bf16[2048,2048]{1,0:T(8,128)(2,1)} %param.21), kind=kOutput, calls=%fused_computation.13 | convolution fusion | flops 1075314560 | bytes 9961984 | tf_op jit(solution)/shard_map/dot_general | solution.py:757
  48.8 0.0 copy-start.1
  48.9 0.0 copy-done.5
  48.9 1.0 fusion.7.hn_ref
  49.9 2.9 %fusion.2 = pred[4,128,128]{2,1,0:T(8,128)(4,1)S(1)} fusion(s32[4,128,8]{2,1,0:T(8,128)S(1)} %get-tuple-element.8), kind=kLoop, calls=%fused_computation.7 | loop fusion | flops 983040 | bytes 81920 | tf_op jit(solution)/shard_map/reduce_or | solution.py:405
  52.8 0.0 copy-done.10
  52.8 0.2 fusion.4
  53.0 0.0 copy-done.7
  53.0 0.0 copy-done.6
  53.0 0.0 copy-done.9
  53.0 0.0 copy-done.11
  53.0 0.8 fusion.1
  53.9 0.0 copy-done.1
  53.9 1.5 copy.27.pick_ref
  55.4 1.5 and_convert_fusion.place_ref
  56.9 0.8 convert_element_type.82
  57.6 0.8 fusion.10.column_expert_ref
  58.4 175.4 %shard_map.164 = bf16[128,2048]{1,0:T(8,128)(2,1)} custom-call(bf16[128,2048]{1,0:T(8,128)(2,1)} %fusion.7.hn_ref, bf16[128,2048]{1,0:T(8,128)(2,1)} %copy-done.1, bf16[1152,512]{1,0:T(8,128)(2,1)} %copy.27.pick_ref, bf16[512,1152]{1,0:T(8,128)(2,1)} %and_convert_fusion.place_ref, f32[512,128]{1,0:T(8,128)} %bitcast.42, ...), custom_call_target="tpu_custom_call" | custom-call | flops 14495514624 | bytes 37748736 | tf_op jit(solution)/shard_map/pallas_call | solution.py:436
  233.8 1.9 copy.37
  (7 shorter events, 0.1 us)
Async XLA Ops:
  1.1 1.0 copy-start
  1.5 1.1 copy-start.3
  2.2 1.0 copy-start.4
  2.2 1.0 copy-start.8
  3.3 40.6 %copy-start.2 = (bf16[128,2048]{1,0:T(8,128)(2,1)S(1)}, bf16[128,2048]{1,0:T(8,128)(2,1)}, u32[]{:S(2)}) copy-start(bf16[128,2048]{1,0:T(8,128)(2,1)} %param.17) | copy-start | bytes 1572868
  43.9 4.9 %copy-start.5 = (f32[2048]{0:T(1024)S(1)}, f32[2048]{0:T(1024)}, u32[]{:S(2)}) copy-start(f32[2048]{0:T(1024)} %param.22) | copy-start | bytes 24580
  44.0 8.8 %copy-start.10 = (bf16[128,128,1]{1,0,2:T(8,128)(2,1)S(1)}, bf16[128,128,1]{1,0,2:T(8,128)(2,1)}, u32[]{:S(2)}) copy-start(bf16[128,128,1]{1,0,2:T(8,128)(2,1)} %constant.65) | copy-start | bytes 98308
  44.0 9.0 %copy-start.7 = (s32[1152]{0:T(1024)S(1)}, s32[1152]{0:T(1024)}, u32[]{:S(2)}) copy-start(s32[1152]{0:T(1024)} %constant.57.clone) | copy-start | bytes 13828
  44.0 9.0 %copy-start.6 = (s32[1152]{0:T(1024)S(1)}, s32[1152]{0:T(1024)}, u32[]{:S(2)}) copy-start(s32[1152]{0:T(1024)} %constant.60.clone) | copy-start | bytes 13828
  44.0 9.0 %copy-start.9 = (s32[512]{0:T(512)S(1)}, s32[512]{0:T(512)}, u32[]{:S(2)}) copy-start(s32[512]{0:T(512)} %constant.59.clone) | copy-start | bytes 6148
  44.0 9.0 %copy-start.11 = (f32[1152]{0:T(1024)S(1)}, f32[1152]{0:T(1024)}, u32[]{:S(2)}) copy-start(f32[1152]{0:T(1024)} %constant.58.clone) | copy-start | bytes 13828
  48.8 5.0 %copy-start.1 = (bf16[128,2048]{1,0:T(8,128)(2,1)}, bf16[128,2048]{1,0:T(8,128)(2,1)S(1)}, u32[]{:S(2)}) copy-start(bf16[128,2048]{1,0:T(8,128)(2,1)S(1)} %get-tuple-element.16.h1_ref) | copy-start | bytes 1572868
